TPU v7x, 32 devices: a whole 2x2x4 slice. The times are simulated.
32 devices in a mesh: grp: 2 (over x), wide: 16 (over z, y, core).
Axes of the slice: x: 2, y: 2, z: 4, core: 2. Of those that a mesh axis runs over, the one named last changes fastest.
Arguments:
- query_maps: bfloat16 [4096, 1024], P(('grp', 'wide')), parts along dimension 0
- source_maps: bfloat16 [4096, 1024], P(('grp', 'wide')), parts along dimension 0
- hubs: int32 [8], P('grp'), parts along dimension 0, may hold values from 0 to 15, as said below
- pick: int32 [32, 2], P(('grp', 'wide')), parts along dimension 0, may hold values from 0 to 3, all different within a row
- weight_first: bfloat16 [16, 1, 3, 3, 3, 3], replicated, may hold values from -0.625 to 0.625
- bias_first: float32 [16], replicated, may hold values from -0.6 to 0.6
- weight_second: bfloat16 [1, 16, 3, 3, 3, 3], replicated, may hold values from -0.15625 to 0.15625
- bias_second: float32 [1], replicated, may hold values from 0 to 0.2
Outputs:
- consensus: float32 [32, 2, 128, 128], P(('grp', 'wide')), parts along dimension 0
There are 2 independent parts, one for each index of `grp`. A program takes and returns all parts, laid end to end along the dimension named above; an argument that names none is the same for every part. Nothing has to cross between parts.
Inputs may be any that keep to these rules, and one draw needn't show every extreme that they name: `hubs`: distinct photo indices of the batch.
All inputs are finite; a program needn't handle non-finite values.
Results may differ from a plain program's by a relative error of at most 0.0063.
Values may be sent and summed in bfloat16 or wider, within the bound.
A program may use at most 64 MiB of HBM per device.

v0:
```python
import jax
import jax.numpy as jnp
from jax import lax
from jax.sharding import PartitionSpec as P

HQ = 4
WQ = 32
HUBS = 4


def spread(value, axis, source):
    kept = jnp.where(lax.axis_index(axis) == source, value, 0).astype(value.dtype)
    return lax.psum(kept, axis)


def conv_volume(volume, kernel):
    padded = jnp.pad(volume, ((1, 1), (0, 0), (0, 0), (0, 0), (0, 0)))
    height = volume.shape[0]
    result = None
    for offset in range(3):
        term = lax.conv_general_dilated(
            padded[offset : offset + height],
            kernel[:, :, offset],
            (1, 1, 1),
            [(1, 1), (1, 1), (1, 1)],
            preferred_element_type=jnp.float32,
        )
        result = term if result is None else result + term
    return result


def consensus_net(matrix, weight_first, bias_first, weight_second, bias_second):
    cells = matrix.shape[0]
    volume = matrix.reshape(HQ, WQ, HQ, WQ)[:, None]
    preact = conv_volume(volume, weight_first) + bias_first[None, :, None, None, None]
    hidden = jax.nn.relu(preact).astype(jnp.bfloat16)
    result = jax.nn.relu(
        conv_volume(hidden, weight_second) + bias_second[None, :, None, None, None]
    )
    return result.reshape(cells, cells)


def scaled_corr(query, sources):
    query_f = query.astype(jnp.float32)
    sources_f = sources.astype(jnp.float32)
    query_rms = jnp.sqrt(jnp.mean(query_f * query_f, axis=-1) + 1e-06)
    source_rms = jnp.sqrt(jnp.mean(sources_f * sources_f, axis=-1) + 1e-06)
    inner = jnp.einsum("ac,jbc->jab", query, sources, preferred_element_type=jnp.float32)
    scale = jnp.sqrt(jnp.float32(query.shape[1]))
    return (inner / (scale * query_rms[None, :, None] * source_rms[:, None, :])).astype(
        jnp.bfloat16
    )


def per_device(
    query_maps, source_maps, hubs, pick, weight_first, bias_first, weight_second, bias_second
):
    owners = pick[0]
    cells, channels = source_maps.shape
    chosen = jnp.zeros((2, cells, channels), jnp.bfloat16)
    for index in range(HUBS):
        arrived = spread(source_maps, "wide", hubs[index])
        chosen = jnp.where((owners == index)[:, None, None], arrived[None], chosen)
    correlation = scaled_corr(query_maps, chosen)
    volumes = jnp.concatenate([correlation, jnp.swapaxes(correlation, 1, 2)], axis=0)

    def filter_one(matrix):
        return consensus_net(matrix, weight_first, bias_first, weight_second, bias_second)

    filtered = lax.map(filter_one, volumes)
    return (filtered[:2] + jnp.swapaxes(filtered[2:], 1, 2))[None]


def solution(mesh):
    return jax.shard_map(
        per_device,
        mesh=mesh,
        in_specs=(
            P(("grp", "wide"), None),
            P(("grp", "wide"), None),
            P("grp"),
            P(("grp", "wide"), None),
            P(),
            P(),
            P(),
            P(),
        ),
        out_specs=P(("grp", "wide"), None, None, None),
        check_vma=False,
    )
```

profile of v0, /device:TPU:31, one launch (start us, length us, event | category | flops | bytes accessed | tf_op | source)
XLA Modules:
  0.0 564.6 jit_solution(4240992218030931366)
XLA Ops:
  14.3 90.6 %all-reduce.5.cloned.1.call-done = (bf16[128,1024]{1,0:T(8,128)(2,1)}, bf16[128,1024]{1,0:T(8,128)(2,1)}, bf16[128,1024]{1,0:T(8,128)(2,1)}, bf16[128,1024]{1,0:T(8,128)(2,1)}) async-done(((bf16[128,1024]{1,0:T(8,128)(2,1)}, bf16[128,1024]{1,0:T(8,128)(2,1)}, bf16[128,1024]{1,0:T(8,128)(2,1)}, bf16[128,1024]{1,0:T(8,128)(2,1)}), (bf16[128,1024]{1,0:T(8,128)(2,1)}, bf16[128,1024]{1,0:T(8,128)(2,1)}, ...) | async-done | bytes 1048592 | tf_op jit(solution)/shard_map/psum | solution.py:13
  108.3 448.3 %while.12 = (s32[]{:T(128)}, f32[4,128,128]{2,1,0:T(8,128)S(1)}, bf16[4,128,128]{2,1,0:T(8,128)(2,1)S(1)}, bf16[16,1,3,3,3,3]{0,5,4,3,2,1:T(4,128)(2,1)S(1)}, f3...) while((s32[]{:T(128)}, f32[4,128,128]{2,1,0:T(8,128)S(1)}, ...), condition=%wide.region_7.8_spmd, body=%wide.region_6.7_spmd.sunk | while | flops 100311040 | bytes 41547692 | solution.py:70
  109.8 6.2 %fusion.91 = f32[32,4,32,5,16]{2,4,3,1,0:T(8,128)} fusion(bf16[1,32,4,32,7]{3,0,4,2,1:T(2,128)(2,1)S(1)} %copy.115, bf16[16,1,3,3,3]{0,4,3,2,1:T(4,128)(2,1)S(1)} %get-tuple-element.216), kind=kOutput, calls=%fused_computation.45.clone.1 | convolution fusion | flops 14438400 | bytes 1368928 | tf_op jit(solution)/shard_map/while/body/eval_jaxpr/conv_general_dilated | solution.py:21
  123.4 9.4 %broadcast_select_fusion.6 = (bf16[32,4,32,5,16]{2,4,3,1,0:T(8,128)(2,1)}, bf16[32,4,32,5,16]{2,4,3,1,0:T(8,128)(2,1)}) fusion(pred[32,5]{0,1:T(8,128)(4,1)S(1)} %get-tuple-element.254, f32[16]{0:T(128)S(1)} %get-tuple-element.250, bf16[1,32,4,32,7]{3,0,4,2,1:T(2,128)(2,1)S(1)} %copy.111, bf16[16,1,3,3,3]{0,4,3,2,1:T(4,128)(2,1)S(1)} %get-tuple-element.213, ...), kind=kOutput, calls=%fused_computation.14.clone.1 | convolution fusion | flops 17387520 | bytes 3990592 | tf_op jit(solution)/shard_map/while/body/eval_jaxpr/conv_general_dilated | solution.py:21
  143.6 10.4 %copy.120 = bf16[16,32,4,32,7]{3,0,4,2,1:T(8,128)(2,1)} copy(bf16[16,32,4,32,7]{1,0,4,3,2:T(8,128)(2,1)} %bitcast.140) | data formatting | bytes 1835008 | tf_op jit(solution)/shard_map/while/body/eval_jaxpr/conv_general_dilated | solution.py:21
  161.4 10.6 %copy.119 = bf16[32,4,32,7,16]{2,4,3,1,0:T(8,128)(2,1)} copy(bf16[32,4,32,7,16]{0,4,3,2,1:T(8,128)(2,1)} %bitcast.139) | data formatting | bytes 1835008 | tf_op jit(solution)/shard_map/while/body/eval_jaxpr/convert_element_type | solution.py:36
  175.1 10.4 %copy.117 = bf16[16,32,4,32,7]{3,0,4,2,1:T(8,128)(2,1)} copy(bf16[16,32,4,32,7]{1,0,4,3,2:T(8,128)(2,1)} %bitcast.141) | data formatting | bytes 1835008 | tf_op jit(solution)/shard_map/while/body/eval_jaxpr/conv_general_dilated | solution.py:21
  185.5 11.0 %convolution_select_fusion.3 = f32[32,4,32,5,1]{2,4,3,1,0:T(1,128)S(1)} fusion(bf16[16,32,4,32,7]{3,0,4,2,1:T(8,128)(2,1)} %copy.117, pred[32,5]{0,1:T(8,128)(4,1)S(1)} %get-tuple-element.254, bf16[1,16,3,3,3]{1,4,3,2,0:T(4,128)(2,1)S(1)} %get-tuple-element.219), kind=kOutput, calls=%fused_computation.23.clone.1 | convolution fusion | flops 14458880 | bytes 1000448 | tf_op jit(solution)/shard_map/while/body/eval_jaxpr/conv_general_dilated | solution.py:21
  196.6 8.9 %convolution_add_fusion.2 = f32[32,4,32,5,1]{2,4,3,1,0:T(1,128)S(1)} fusion(f32[32,4,32,5,1]{2,4,3,1,0:T(1,128)S(1)} %convolution_select_fusion.3, bf16[32,4,32,7,16]{2,4,3,1,0:T(8,128)(2,1)S(1)} %copy-done.2, bf16[1,16,3,3,3]{1,4,3,2,0:T(4,128)(2,1)S(1)} %get-tuple-element.223), kind=kOutput, calls=%fused_computation.18.clone.1 | convolution fusion | flops 14458880 | bytes 1082208 | tf_op jit(solution)/shard_map/while/body/eval_jaxpr/conv_general_dilated | solution.py:21
  205.5 9.8 %fusion.97 = f32[32,4,32,5,1]{2,4,3,1,0:T(1,128)S(1)} fusion(f32[32,4,32,5,1]{2,4,3,1,0:T(1,128)S(1)} %convolution_add_fusion.2, bf16[16,32,4,32,7]{3,0,4,2,1:T(8,128)(2,1)S(1)} %copy-done.1, pred[32,5]{0,1:T(8,128)(4,1)S(1)} %get-tuple-element.254, f32[]{:T(128)} %bitcast.137, bf16[1,16,3,3,3]{1,4,3,2,0:T(4,128)(2,1)S(1)} %get-tuple-element.225), kind=kOutput, calls=%fused_computation.22.clone.1 | convolution fusion | flops 14520320 | bytes 1082372 | tf_op jit(solution)/shard_map/while/body/eval_jaxpr/conv_general_dilated | solution.py:21
  235.5 9.4 %broadcast_select_fusion.6 = (bf16[32,4,32,5,16]{2,4,3,1,0:T(8,128)(2,1)}, bf16[32,4,32,5,16]{2,4,3,1,0:T(8,128)(2,1)}) fusion(pred[32,5]{0,1:T(8,128)(4,1)S(1)} %get-tuple-element.254, f32[16]{0:T(128)S(1)} %get-tuple-element.250, bf16[1,32,4,32,7]{3,0,4,2,1:T(2,128)(2,1)S(1)} %copy.111, bf16[16,1,3,3,3]{0,4,3,2,1:T(4,128)(2,1)S(1)} %get-tuple-element.213, ...), kind=kOutput, calls=%fused_computation.14.clone.1 | convolution fusion | flops 17387520 | bytes 3990592 | tf_op jit(solution)/shard_map/while/body/eval_jaxpr/conv_general_dilated | solution.py:21
  255.2 10.4 %copy.120 = bf16[16,32,4,32,7]{3,0,4,2,1:T(8,128)(2,1)} copy(bf16[16,32,4,32,7]{1,0,4,3,2:T(8,128)(2,1)} %bitcast.140) | data formatting | bytes 1835008 | tf_op jit(solution)/shard_map/while/body/eval_jaxpr/conv_general_dilated | solution.py:21
  273.1 10.6 %copy.119 = bf16[32,4,32,7,16]{2,4,3,1,0:T(8,128)(2,1)} copy(bf16[32,4,32,7,16]{0,4,3,2,1:T(8,128)(2,1)} %bitcast.139) | data formatting | bytes 1835008 | tf_op jit(solution)/shard_map/while/body/eval_jaxpr/convert_element_type | solution.py:36
  286.7 10.4 %copy.117 = bf16[16,32,4,32,7]{3,0,4,2,1:T(8,128)(2,1)} copy(bf16[16,32,4,32,7]{1,0,4,3,2:T(8,128)(2,1)} %bitcast.141) | data formatting | bytes 1835008 | tf_op jit(solution)/shard_map/while/body/eval_jaxpr/conv_general_dilated | solution.py:21
  297.2 11.1 %convolution_select_fusion.3 = f32[32,4,32,5,1]{2,4,3,1,0:T(1,128)S(1)} fusion(bf16[16,32,4,32,7]{3,0,4,2,1:T(8,128)(2,1)} %copy.117, pred[32,5]{0,1:T(8,128)(4,1)S(1)} %get-tuple-element.254, bf16[1,16,3,3,3]{1,4,3,2,0:T(4,128)(2,1)S(1)} %get-tuple-element.219), kind=kOutput, calls=%fused_computation.23.clone.1 | convolution fusion | flops 14458880 | bytes 1000448 | tf_op jit(solution)/shard_map/while/body/eval_jaxpr/conv_general_dilated | solution.py:21
  308.3 8.9 %convolution_add_fusion.2 = f32[32,4,32,5,1]{2,4,3,1,0:T(1,128)S(1)} fusion(f32[32,4,32,5,1]{2,4,3,1,0:T(1,128)S(1)} %convolution_select_fusion.3, bf16[32,4,32,7,16]{2,4,3,1,0:T(8,128)(2,1)S(1)} %copy-done.2, bf16[1,16,3,3,3]{1,4,3,2,0:T(4,128)(2,1)S(1)} %get-tuple-element.223), kind=kOutput, calls=%fused_computation.18.clone.1 | convolution fusion | flops 14458880 | bytes 1082208 | tf_op jit(solution)/shard_map/while/body/eval_jaxpr/conv_general_dilated | solution.py:21
  317.2 10.0 %fusion.97 = f32[32,4,32,5,1]{2,4,3,1,0:T(1,128)S(1)} fusion(f32[32,4,32,5,1]{2,4,3,1,0:T(1,128)S(1)} %convolution_add_fusion.2, bf16[16,32,4,32,7]{3,0,4,2,1:T(8,128)(2,1)S(1)} %copy-done.1, pred[32,5]{0,1:T(8,128)(4,1)S(1)} %get-tuple-element.254, f32[]{:T(128)} %bitcast.137, bf16[1,16,3,3,3]{1,4,3,2,0:T(4,128)(2,1)S(1)} %get-tuple-element.225), kind=kOutput, calls=%fused_computation.22.clone.1 | convolution fusion | flops 14520320 | bytes 1082372 | tf_op jit(solution)/shard_map/while/body/eval_jaxpr/conv_general_dilated | solution.py:21
  333.4 6.2 %fusion.91 = f32[32,4,32,5,16]{2,4,3,1,0:T(8,128)} fusion(bf16[1,32,4,32,7]{3,0,4,2,1:T(2,128)(2,1)S(1)} %copy.115, bf16[16,1,3,3,3]{0,4,3,2,1:T(4,128)(2,1)S(1)} %get-tuple-element.216), kind=kOutput, calls=%fused_computation.45.clone.1 | convolution fusion | flops 14438400 | bytes 1368928 | tf_op jit(solution)/shard_map/while/body/eval_jaxpr/conv_general_dilated | solution.py:21
  347.1 9.4 %broadcast_select_fusion.6 = (bf16[32,4,32,5,16]{2,4,3,1,0:T(8,128)(2,1)}, bf16[32,4,32,5,16]{2,4,3,1,0:T(8,128)(2,1)}) fusion(pred[32,5]{0,1:T(8,128)(4,1)S(1)} %get-tuple-element.254, f32[16]{0:T(128)S(1)} %get-tuple-element.250, bf16[1,32,4,32,7]{3,0,4,2,1:T(2,128)(2,1)S(1)} %copy.111, bf16[16,1,3,3,3]{0,4,3,2,1:T(4,128)(2,1)S(1)} %get-tuple-element.213, ...), kind=kOutput, calls=%fused_computation.14.clone.1 | convolution fusion | flops 17387520 | bytes 3990592 | tf_op jit(solution)/shard_map/while/body/eval_jaxpr/conv_general_dilated | solution.py:21
  366.9 10.4 %copy.120 = bf16[16,32,4,32,7]{3,0,4,2,1:T(8,128)(2,1)} copy(bf16[16,32,4,32,7]{1,0,4,3,2:T(8,128)(2,1)} %bitcast.140) | data formatting | bytes 1835008 | tf_op jit(solution)/shard_map/while/body/eval_jaxpr/conv_general_dilated | solution.py:21
  384.8 10.6 %copy.119 = bf16[32,4,32,7,16]{2,4,3,1,0:T(8,128)(2,1)} copy(bf16[32,4,32,7,16]{0,4,3,2,1:T(8,128)(2,1)} %bitcast.139) | data formatting | bytes 1835008 | tf_op jit(solution)/shard_map/while/body/eval_jaxpr/convert_element_type | solution.py:36
  398.4 10.4 %copy.117 = bf16[16,32,4,32,7]{3,0,4,2,1:T(8,128)(2,1)} copy(bf16[16,32,4,32,7]{1,0,4,3,2:T(8,128)(2,1)} %bitcast.141) | data formatting | bytes 1835008 | tf_op jit(solution)/shard_map/while/body/eval_jaxpr/conv_general_dilated | solution.py:21
  408.9 11.2 %convolution_select_fusion.3 = f32[32,4,32,5,1]{2,4,3,1,0:T(1,128)S(1)} fusion(bf16[16,32,4,32,7]{3,0,4,2,1:T(8,128)(2,1)} %copy.117, pred[32,5]{0,1:T(8,128)(4,1)S(1)} %get-tuple-element.254, bf16[1,16,3,3,3]{1,4,3,2,0:T(4,128)(2,1)S(1)} %get-tuple-element.219), kind=kOutput, calls=%fused_computation.23.clone.1 | convolution fusion | flops 14458880 | bytes 1000448 | tf_op jit(solution)/shard_map/while/body/eval_jaxpr/conv_general_dilated | solution.py:21
  420.2 8.9 %convolution_add_fusion.2 = f32[32,4,32,5,1]{2,4,3,1,0:T(1,128)S(1)} fusion(f32[32,4,32,5,1]{2,4,3,1,0:T(1,128)S(1)} %convolution_select_fusion.3, bf16[32,4,32,7,16]{2,4,3,1,0:T(8,128)(2,1)S(1)} %copy-done.2, bf16[1,16,3,3,3]{1,4,3,2,0:T(4,128)(2,1)S(1)} %get-tuple-element.223), kind=kOutput, calls=%fused_computation.18.clone.1 | convolution fusion | flops 14458880 | bytes 1082208 | tf_op jit(solution)/shard_map/while/body/eval_jaxpr/conv_general_dilated | solution.py:21
  429.1 9.7 %fusion.97 = f32[32,4,32,5,1]{2,4,3,1,0:T(1,128)S(1)} fusion(f32[32,4,32,5,1]{2,4,3,1,0:T(1,128)S(1)} %convolution_add_fusion.2, bf16[16,32,4,32,7]{3,0,4,2,1:T(8,128)(2,1)S(1)} %copy-done.1, pred[32,5]{0,1:T(8,128)(4,1)S(1)} %get-tuple-element.254, f32[]{:T(128)} %bitcast.137, bf16[1,16,3,3,3]{1,4,3,2,0:T(4,128)(2,1)S(1)} %get-tuple-element.225), kind=kOutput, calls=%fused_computation.22.clone.1 | convolution fusion | flops 14520320 | bytes 1082372 | tf_op jit(solution)/shard_map/while/body/eval_jaxpr/conv_general_dilated | solution.py:21
  458.8 9.4 %broadcast_select_fusion.6 = (bf16[32,4,32,5,16]{2,4,3,1,0:T(8,128)(2,1)}, bf16[32,4,32,5,16]{2,4,3,1,0:T(8,128)(2,1)}) fusion(pred[32,5]{0,1:T(8,128)(4,1)S(1)} %get-tuple-element.254, f32[16]{0:T(128)S(1)} %get-tuple-element.250, bf16[1,32,4,32,7]{3,0,4,2,1:T(2,128)(2,1)S(1)} %copy.111, bf16[16,1,3,3,3]{0,4,3,2,1:T(4,128)(2,1)S(1)} %get-tuple-element.213, ...), kind=kOutput, calls=%fused_computation.14.clone.1 | convolution fusion | flops 17387520 | bytes 3990592 | tf_op jit(solution)/shard_map/while/body/eval_jaxpr/conv_general_dilated | solution.py:21
  478.8 10.4 %copy.120 = bf16[16,32,4,32,7]{3,0,4,2,1:T(8,128)(2,1)} copy(bf16[16,32,4,32,7]{1,0,4,3,2:T(8,128)(2,1)} %bitcast.140) | data formatting | bytes 1835008 | tf_op jit(solution)/shard_map/while/body/eval_jaxpr/conv_general_dilated | solution.py:21
  496.7 10.6 %copy.119 = bf16[32,4,32,7,16]{2,4,3,1,0:T(8,128)(2,1)} copy(bf16[32,4,32,7,16]{0,4,3,2,1:T(8,128)(2,1)} %bitcast.139) | data formatting | bytes 1835008 | tf_op jit(solution)/shard_map/while/body/eval_jaxpr/convert_element_type | solution.py:36
  510.3 10.4 %copy.117 = bf16[16,32,4,32,7]{3,0,4,2,1:T(8,128)(2,1)} copy(bf16[16,32,4,32,7]{1,0,4,3,2:T(8,128)(2,1)} %bitcast.141) | data formatting | bytes 1835008 | tf_op jit(solution)/shard_map/while/body/eval_jaxpr/conv_general_dilated | solution.py:21
  520.8 11.0 %convolution_select_fusion.3 = f32[32,4,32,5,1]{2,4,3,1,0:T(1,128)S(1)} fusion(bf16[16,32,4,32,7]{3,0,4,2,1:T(8,128)(2,1)} %copy.117, pred[32,5]{0,1:T(8,128)(4,1)S(1)} %get-tuple-element.254, bf16[1,16,3,3,3]{1,4,3,2,0:T(4,128)(2,1)S(1)} %get-tuple-element.219), kind=kOutput, calls=%fused_computation.23.clone.1 | convolution fusion | flops 14458880 | bytes 1000448 | tf_op jit(solution)/shard_map/while/body/eval_jaxpr/conv_general_dilated | solution.py:21
  531.8 8.9 %convolution_add_fusion.2 = f32[32,4,32,5,1]{2,4,3,1,0:T(1,128)S(1)} fusion(f32[32,4,32,5,1]{2,4,3,1,0:T(1,128)S(1)} %convolution_select_fusion.3, bf16[32,4,32,7,16]{2,4,3,1,0:T(8,128)(2,1)S(1)} %copy-done.2, bf16[1,16,3,3,3]{1,4,3,2,0:T(4,128)(2,1)S(1)} %get-tuple-element.223), kind=kOutput, calls=%fused_computation.18.clone.1 | convolution fusion | flops 14458880 | bytes 1082208 | tf_op jit(solution)/shard_map/while/body/eval_jaxpr/conv_general_dilated | solution.py:21
  540.8 9.8 %fusion.97 = f32[32,4,32,5,1]{2,4,3,1,0:T(1,128)S(1)} fusion(f32[32,4,32,5,1]{2,4,3,1,0:T(1,128)S(1)} %convolution_add_fusion.2, bf16[16,32,4,32,7]{3,0,4,2,1:T(8,128)(2,1)S(1)} %copy-done.1, pred[32,5]{0,1:T(8,128)(4,1)S(1)} %get-tuple-element.254, f32[]{:T(128)} %bitcast.137, bf16[1,16,3,3,3]{1,4,3,2,0:T(4,128)(2,1)S(1)} %get-tuple-element.225), kind=kOutput, calls=%fused_computation.22.clone.1 | convolution fusion | flops 14520320 | bytes 1082372 | tf_op jit(solution)/shard_map/while/body/eval_jaxpr/conv_general_dilated | solution.py:21
  (208 shorter events, 143.7 us)
Async XLA Ops:
  6.5 99.9 %copy-start.5 = (bf16[128,1024]{1,0:T(8,128)(2,1)S(1)}, bf16[128,1024]{1,0:T(8,128)(2,1)}, u32[]{:S(2)}) copy-start(bf16[128,1024]{1,0:T(8,128)(2,1)} %param.10) | copy-start | bytes 786436
  6.5 98.3 %all-reduce.5.cloned.1.call-start = ((), (), s32[]{:S(2)}) async-start(), calls=%async_computation | async-start | bytes 2097152 | tf_op jit(solution)/shard_map/psum | solution.py:13
  10.4 97.9 %copy-start.3 = (bf16[16,1,3,3,3,3]{0,5,4,3,2,1:T(4,128)(2,1)S(1)}, bf16[16,1,3,3,3,3]{0,5,4,3,2,1:T(4,128)(2,1)}, u32[]{:S(2)}) copy-start(bf16[16,1,3,3,3,3]{0,5,4,3,2,1:T(4,128)(2,1)} %param.14) | copy-start | bytes 7780
  10.5 97.9 %copy-start.4 = (bf16[1,16,3,3,3,3]{1,5,4,3,2,0:T(4,128)(2,1)S(1)}, bf16[1,16,3,3,3,3]{1,5,4,3,2,0:T(4,128)(2,1)}, u32[]{:S(2)}) copy-start(bf16[1,16,3,3,3,3]{1,5,4,3,2,0:T(4,128)(2,1)} %param.16) | copy-start | bytes 7780
  10.5 97.9 %copy-start.6 = (f32[16]{0:T(128)S(1)}, f32[16]{0:T(128)}, u32[]{:S(2)}) copy-start(f32[16]{0:T(128)} %param.15) | copy-start | bytes 196
  10.5 97.9 %copy-start.7 = (pred[32,5]{0,1:T(8,128)(4,1)S(1)}, pred[32,5]{0,1:T(8,128)(4,1)}, u32[]{:S(2)}) copy-start(pred[32,5]{0,1:T(8,128)(4,1)} %constant.157) | copy-start | bytes 484
  161.4 10.6 %copy-start = (bf16[16,32,4,4,32]{1,0,4,3,2:T(8,128)(2,1)S(1)}, bf16[16,32,4,4,32]{1,0,4,3,2:T(8,128)(2,1)}, u32[]{:S(2)}) copy-start(bf16[16,32,4,4,32]{1,0,4,3,2:T(8,128)(2,1)} %get-tuple-element.218) | copy-start | bytes 1572868 | tf_op jit(solution)/shard_map/while
  185.5 11.0 %copy-start.2 = (bf16[32,4,32,7,16]{2,4,3,1,0:T(8,128)(2,1)S(1)}, bf16[32,4,32,7,16]{2,4,3,1,0:T(8,128)(2,1)}, u32[]{:S(2)}) copy-start(bf16[32,4,32,7,16]{2,4,3,1,0:T(8,128)(2,1)} %copy.119) | copy-start | bytes 2752516 | tf_op jit(solution)/shard_map/while
  196.5 9.0 %copy-start.1 = (bf16[16,32,4,32,7]{3,0,4,2,1:T(8,128)(2,1)S(1)}, bf16[16,32,4,32,7]{3,0,4,2,1:T(8,128)(2,1)}, u32[]{:S(2)}) copy-start(bf16[16,32,4,32,7]{3,0,4,2,1:T(8,128)(2,1)} %copy.120) | copy-start | bytes 2752516 | tf_op jit(solution)/shard_map/while
  273.1 10.6 %copy-start = (bf16[16,32,4,4,32]{1,0,4,3,2:T(8,128)(2,1)S(1)}, bf16[16,32,4,4,32]{1,0,4,3,2:T(8,128)(2,1)}, u32[]{:S(2)}) copy-start(bf16[16,32,4,4,32]{1,0,4,3,2:T(8,128)(2,1)} %get-tuple-element.218) | copy-start | bytes 1572868 | tf_op jit(solution)/shard_map/while
  297.2 11.1 %copy-start.2 = (bf16[32,4,32,7,16]{2,4,3,1,0:T(8,128)(2,1)S(1)}, bf16[32,4,32,7,16]{2,4,3,1,0:T(8,128)(2,1)}, u32[]{:S(2)}) copy-start(bf16[32,4,32,7,16]{2,4,3,1,0:T(8,128)(2,1)} %copy.119) | copy-start | bytes 2752516 | tf_op jit(solution)/shard_map/while
  308.2 9.0 %copy-start.1 = (bf16[16,32,4,32,7]{3,0,4,2,1:T(8,128)(2,1)S(1)}, bf16[16,32,4,32,7]{3,0,4,2,1:T(8,128)(2,1)}, u32[]{:S(2)}) copy-start(bf16[16,32,4,32,7]{3,0,4,2,1:T(8,128)(2,1)} %copy.120) | copy-start | bytes 2752516 | tf_op jit(solution)/shard_map/while
  384.8 10.6 %copy-start = (bf16[16,32,4,4,32]{1,0,4,3,2:T(8,128)(2,1)S(1)}, bf16[16,32,4,4,32]{1,0,4,3,2:T(8,128)(2,1)}, u32[]{:S(2)}) copy-start(bf16[16,32,4,4,32]{1,0,4,3,2:T(8,128)(2,1)} %get-tuple-element.218) | copy-start | bytes 1572868 | tf_op jit(solution)/shard_map/while
  408.9 11.3 %copy-start.2 = (bf16[32,4,32,7,16]{2,4,3,1,0:T(8,128)(2,1)S(1)}, bf16[32,4,32,7,16]{2,4,3,1,0:T(8,128)(2,1)}, u32[]{:S(2)}) copy-start(bf16[32,4,32,7,16]{2,4,3,1,0:T(8,128)(2,1)} %copy.119) | copy-start | bytes 2752516 | tf_op jit(solution)/shard_map/while
  420.1 9.0 %copy-start.1 = (bf16[16,32,4,32,7]{3,0,4,2,1:T(8,128)(2,1)S(1)}, bf16[16,32,4,32,7]{3,0,4,2,1:T(8,128)(2,1)}, u32[]{:S(2)}) copy-start(bf16[16,32,4,32,7]{3,0,4,2,1:T(8,128)(2,1)} %copy.120) | copy-start | bytes 2752516 | tf_op jit(solution)/shard_map/while
  496.7 10.6 %copy-start = (bf16[16,32,4,4,32]{1,0,4,3,2:T(8,128)(2,1)S(1)}, bf16[16,32,4,4,32]{1,0,4,3,2:T(8,128)(2,1)}, u32[]{:S(2)}) copy-start(bf16[16,32,4,4,32]{1,0,4,3,2:T(8,128)(2,1)} %get-tuple-element.218) | copy-start | bytes 1572868 | tf_op jit(solution)/shard_map/while
  520.8 11.0 %copy-start.2 = (bf16[32,4,32,7,16]{2,4,3,1,0:T(8,128)(2,1)S(1)}, bf16[32,4,32,7,16]{2,4,3,1,0:T(8,128)(2,1)}, u32[]{:S(2)}) copy-start(bf16[32,4,32,7,16]{2,4,3,1,0:T(8,128)(2,1)} %copy.119) | copy-start | bytes 2752516 | tf_op jit(solution)/shard_map/while
  531.8 9.0 %copy-start.1 = (bf16[16,32,4,32,7]{3,0,4,2,1:T(8,128)(2,1)S(1)}, bf16[16,32,4,32,7]{3,0,4,2,1:T(8,128)(2,1)}, u32[]{:S(2)}) copy-start(bf16[16,32,4,32,7]{3,0,4,2,1:T(8,128)(2,1)} %copy.120) | copy-start | bytes 2752516 | tf_op jit(solution)/shard_map/while
Sparse Core Ops, SparseCore 0:
  12.6 92.1 all-reduce.4
where the time goes:
time: 572 us; the launch traced here: 565 us
  matrix products  207 us (36%)
  local copies, waits for them, and re-layouts  196 us (34%)
  waiting for transfers between devices  90.6 us (16%)
  other arithmetic  35.3 us (6%)
  loops' own time  19.4 us (3%)
  between operations  16.3 us (3%)
    conv_general_dilated x24, matrix products, conv_volume(): lax.conv_general_dilated(padded[offset:offset + height], kernel[:, :, off...  206 us
    psum x1, waiting for transfers between devices, spread(): return lax.psum(kept, axis)  90.6 us
    conv_general_dilated x52, local copies, waits for them, and re-layouts, conv_volume(): lax.conv_general_dilated(padded[offset:offset + height], kernel[:, :, off...  89.9 us
    convert_element_type x20, local copies, waits for them, and re-layouts, consensus_net(): hidden = jax.nn.relu(preact).astype(jnp.bfloat16)  85.4 us
    conv_general_dilated x20, other arithmetic, conv_volume(): lax.conv_general_dilated(padded[offset:offset + height], kernel[:, :, off...  19.8 us
    another operation x1, loops' own time, per_device(): filtered = lax.map(filter_one, volumes)  19.4 us
    slice x24, local copies, waits for them, and re-layouts, conv_volume(): padded[offset:offset + height]  13.8 us
  transfers between devices with their start and end apart: 1, of which 1 were waited for; matrix products, arithmetic and copies ran while one was open for 0% of the time, Pallas kernels for 0%

commit v1 on v0

v1 whole, which is shorter than its diff:
```python
import functools

import jax
import jax.numpy as jnp
from jax import lax
from jax.experimental import pallas as pl
from jax.experimental.pallas import tpu as pltpu
from jax.sharding import PartitionSpec as P

HQ = 4
WQ = 32
CELLS = HQ * WQ
HID = 16
TAPS = 9
NETS = 4
ROWS16 = 16
OFFSETS = [(i, j) for i in (-1, 0, 1) for j in (-1, 0, 1)]


def iota(shape, dim):
    return lax.broadcasted_iota(jnp.int32, shape, dim)


def tap_vectors(taps_ref, v_ref):
    row, lane = iota((128, CELLS), 0), iota((128, CELLS), 1)
    place = jnp.zeros((128, CELLS), jnp.bool_)
    for t, (i, j) in enumerate(OFFSETS):
        place |= (row == t) & (lane == (-(WQ * i + j)) % CELLS)
    spread = jnp.where(place, 1.0, 0.0).astype(jnp.bfloat16)
    v_ref[...] = jnp.dot(taps_ref[...], spread, preferred_element_type=jnp.float32)


def band_mask():
    cin, cout = iota((CELLS, CELLS), 0), iota((CELLS, CELLS), 1)
    rows = jnp.abs((cin >> 5) - (cout >> 5)) <= 1
    columns = jnp.abs((cin & (WQ - 1)) - (cout & (WQ - 1))) <= 1
    return jnp.where(rows & columns, 1.0, 0.0)


def band(v_ref, index, mask):
    line = jnp.broadcast_to(v_ref[pl.ds(index, 1), :], (CELLS, CELLS))
    return (pltpu.roll(line, 0, 1, stride=1, stride_axis=0) * mask).astype(jnp.bfloat16)


def build_first(v_ref, w_ref):
    mask = band_mask()

    def body(o, _):
        for d in range(TAPS):
            w_ref[pl.ds(d * CELLS, CELLS), pl.ds(pl.multiple_of(o * CELLS, CELLS), CELLS)] = band(
                v_ref, o * TAPS + d, mask
            )
        return 0

    lax.fori_loop(0, HID, body, 0)


def build_second(v_ref, w_ref):
    mask = band_mask()

    def body(o, _):
        for d in range(TAPS):
            w_ref[pl.ds(pl.multiple_of(o * CELLS, CELLS), CELLS), pl.ds(d * CELLS, CELLS)] = band(
                v_ref, HID * TAPS + o * TAPS + d, mask
            )
        return 0

    lax.fori_loop(0, HID, body, 0)


def column_shift(value, j):
    if j == 0:
        return value
    rows = value.shape[0]
    column = iota(value.shape, 0) & (WQ - 1)
    moved = pltpu.roll(value, (-j) % rows, 0)
    inside = column < WQ - 1 if j > 0 else column > 0
    return jnp.where(inside, moved, 0.0)


def row_pieces(i):
    if i == 0:
        return (0, CELLS), (0, CELLS), None
    if i < 0:
        return (WQ, CELLS), (0, CELLS - WQ), (0, WQ)
    return (0, CELLS - WQ), (WQ, CELLS), (CELLS - WQ, CELLS)


def correlate(q_ref, chosen, pair):
    query, source = q_ref[...], chosen[pair]
    channels = query.shape[1]
    qf, sf = query.astype(jnp.float32), source.astype(jnp.float32)
    rq = jnp.sqrt(jnp.sum(qf * qf, axis=1, keepdims=True) / channels + 1e-06)
    rs = jnp.sqrt(jnp.sum(sf * sf, axis=1, keepdims=True) / channels + 1e-06)
    rs = jnp.broadcast_to(rs, (CELLS, CELLS)).T
    inner = lax.dot_general(
        query, source, (((1,), (1,)), ((), ())), preferred_element_type=jnp.float32
    )
    corr = inner / (jnp.sqrt(jnp.float32(channels)) * rq * rs)
    return corr.astype(jnp.bfloat16).astype(jnp.float32)


def fill_shifted(x_ref, net, matrix):
    base = net * CELLS
    for jn, j in enumerate((-1, 0, 1)):
        moved = column_shift(matrix, j).astype(jnp.bfloat16)
        for im, i in enumerate((-1, 0, 1)):
            d = im * 3 + jn
            (w0, w1), (r0, r1), gap = row_pieces(i)
            x_ref[base + w0 : base + w1, d * CELLS : (d + 1) * CELLS] = moved[r0:r1]
            if gap is not None:
                x_ref[base + gap[0] : base + gap[1], d * CELLS : (d + 1) * CELLS] = jnp.zeros(
                    (WQ, CELLS), jnp.bfloat16
                )


def first_conv(x_ref, w_ref, b_ref, h_ref):
    def body(c, _):
        at = pl.ds(pl.multiple_of(c * 256, 256), 256)
        acc = jnp.dot(x_ref[...], w_ref[:, at], preferred_element_type=jnp.float32)
        lane = iota((1, 256), 1)
        bias = jnp.where(lane < CELLS, b_ref[2 * c], b_ref[2 * c + 1])
        h_ref[:, at] = jnp.maximum(acc + bias, 0.0).astype(jnp.bfloat16)
        return 0

    lax.fori_loop(0, HID * CELLS // 256, body, 0)


def second_conv(h_ref, w_ref, y_ref):
    def body(c, _):
        at = pl.ds(pl.multiple_of(c * 256, 256), 256)
        y_ref[:, at] = jnp.dot(h_ref[...], w_ref[:, at], preferred_element_type=jnp.float32)
        return 0

    lax.fori_loop(0, TAPS * CELLS // 256, body, 0)
    rest = TAPS * CELLS // 256 * 256
    y_ref[:, rest:] = jnp.dot(h_ref[...], w_ref[:, rest:], preferred_element_type=jnp.float32)


def combine(y_ref, net, bias):
    base = net * CELLS
    total = None
    for jn, j in enumerate((-1, 0, 1)):
        part = []
        for r in range(HQ):
            piece = None
            for im, i in enumerate((-1, 0, 1)):
                if 0 <= r + i < HQ:
                    d = im * 3 + jn
                    start = base + (r + i) * WQ
                    term = y_ref[start : start + WQ, d * CELLS : (d + 1) * CELLS]
                    piece = term if piece is None else piece + term
            part.append(piece)
        term = column_shift(jnp.concatenate(part, axis=0), j)
        total = term if total is None else total + term
    return jnp.maximum(total + bias, 0.0)


def kernel(
    n, q_ref, s_ref, hubs_ref, pick_ref, taps_ref, b1_ref, b2_ref, out_ref,
    stage, mine, owners, outbox, chosen, v, w1, w2, x, h, y,
    send1, recv1, sendo, recvo, send2, recv2, local,
):
    me = lax.axis_index("wide")
    across = n // (CELLS // ROWS16)
    width = s_ref.shape[1] // across

    def piece(index):
        return (
            pl.ds(pl.multiple_of((index // across) * ROWS16, ROWS16), ROWS16),
            pl.ds(pl.multiple_of((index % across) * width, width), width),
        )

    def peers(body):
        def step(s, _):
            body(lax.rem(me + s, n))
            return 0

        lax.fori_loop(1, n, step, 0)

    barrier = pltpu.get_barrier_semaphore()
    peers(lambda p: pl.semaphore_signal(
        barrier, inc=1, device_id={"wide": p}, device_id_type=pl.DeviceIdType.MESH))

    row = iota((8, 128), 0)
    mine[...] = jnp.where(row < 4, hubs_ref[pick_ref[0, 0]], hubs_ref[pick_ref[0, 1]])
    own_rows, own_columns = piece(me)
    keep = pltpu.make_async_copy(s_ref.at[own_rows, own_columns], stage.at[me], local.at[0])
    keep.start()
    pl.semaphore_wait(barrier, n - 1)

    def scatter(p, slot):
        rows, columns = piece(p)
        return pltpu.make_async_remote_copy(
            src_ref=s_ref.at[rows, columns], dst_ref=stage.at[slot],
            send_sem=send1.at[p], recv_sem=recv1.at[slot],
            device_id={"wide": p}, device_id_type=pl.DeviceIdType.MESH)

    def tell(p, slot):
        return pltpu.make_async_remote_copy(
            src_ref=mine, dst_ref=owners.at[slot],
            send_sem=sendo.at[p], recv_sem=recvo.at[slot],
            device_id={"wide": p}, device_id_type=pl.DeviceIdType.MESH)

    def deliver(p, slot):
        rows, columns = piece(slot)
        return pltpu.make_async_remote_copy(
            src_ref=outbox.at[p], dst_ref=chosen.at[:, rows, columns],
            send_sem=send2.at[p], recv_sem=recv2.at[slot],
            device_id={"wide": p}, device_id_type=pl.DeviceIdType.MESH)

    def start_first(p):
        tell(p, me).start()
        scatter(p, me).start()

    peers(start_first)
    owners[me] = mine[...]
    tap_vectors(taps_ref, v)
    build_first(v, w1)
    keep.wait()

    def wait_first(p):
        tell(p, p).wait_recv()
        scatter(p, p).wait_recv()

    peers(wait_first)

    def pack(p):
        outbox[p, 0] = stage[owners[p, 0, 0]]
        outbox[p, 1] = stage[owners[p, 4, 0]]

    def send_second(p):
        pack(p)
        deliver(p, me).start()

    peers(send_second)
    pack(me)
    stay = pltpu.make_async_copy(
        outbox.at[me], chosen.at[:, own_rows, own_columns], local.at[1])
    stay.start()
    build_second(v, w2)
    stay.wait()
    peers(lambda p: deliver(p, p).wait_recv())

    for pair in range(2):
        corr = correlate(q_ref, chosen, pair)
        fill_shifted(x, pair, corr)
        fill_shifted(x, 2 + pair, corr.T)
    first_conv(x, w1, b1_ref, h)
    second_conv(h, w2, y)
    for pair in range(2):
        forward = combine(y, pair, b2_ref[0])
        backward = combine(y, 2 + pair, b2_ref[0])
        out_ref[0, pair] = forward + backward.T

    def wait_sent(p):
        tell(p, me).wait_send()
        scatter(p, me).wait_send()
        deliver(p, me).wait_send()

    peers(wait_sent)


def per_device(
    n, query_maps, source_maps, hubs, pick, weight_first, bias_first, weight_second, bias_second
):
    cells, channels = source_maps.shape
    taps = jnp.concatenate(
        [weight_first.reshape(HID * TAPS, TAPS), weight_second.reshape(HID * TAPS, TAPS)], axis=0
    )
    taps = jnp.pad(taps, ((0, 0), (0, 128 - TAPS)))
    width = channels // (n // (cells // ROWS16))
    vmem = pl.BlockSpec(memory_space=pltpu.VMEM)
    smem = pl.BlockSpec(memory_space=pltpu.SMEM)
    return pl.pallas_call(
        functools.partial(kernel, n),
        out_shape=jax.ShapeDtypeStruct((1, 2, cells, cells), jnp.float32),
        in_specs=[vmem, pl.BlockSpec(memory_space=pl.ANY), smem, smem, vmem, smem, smem],
        out_specs=vmem,
        scratch_shapes=[
            pltpu.VMEM((n, ROWS16, width), jnp.bfloat16),
            pltpu.VMEM((8, 128), jnp.int32),
            pltpu.VMEM((n, 8, 128), jnp.int32),
            pltpu.VMEM((n, 2, ROWS16, width), jnp.bfloat16),
            pltpu.VMEM((2, cells, channels), jnp.bfloat16),
            pltpu.VMEM((2 * HID * TAPS, CELLS), jnp.float32),
            pltpu.VMEM((TAPS * CELLS, HID * CELLS), jnp.bfloat16),
            pltpu.VMEM((HID * CELLS, TAPS * CELLS), jnp.bfloat16),
            pltpu.VMEM((NETS * CELLS, TAPS * CELLS), jnp.bfloat16),
            pltpu.VMEM((NETS * CELLS, HID * CELLS), jnp.bfloat16),
            pltpu.VMEM((NETS * CELLS, TAPS * CELLS), jnp.float32),
        ]
        + [pltpu.SemaphoreType.DMA((n,))] * 6
        + [pltpu.SemaphoreType.DMA((2,))],
        compiler_params=pltpu.CompilerParams(
            collective_id=0, has_side_effects=True, vmem_limit_bytes=40 * 1024 * 1024
        ),
        name="consensus",
    )(query_maps, source_maps, hubs, pick, taps, bias_first, bias_second)


def solution(mesh):
    return jax.shard_map(
        functools.partial(per_device, mesh.shape["wide"]),
        mesh=mesh,
        in_specs=(
            P(("grp", "wide"), None),
            P(("grp", "wide"), None),
            P("grp"),
            P(("grp", "wide"), None),
            P(),
            P(),
            P(),
            P(),
        ),
        out_specs=P(("grp", "wide"), None, None, None),
        check_vma=False,
    )
```

time: 572 us -> 39.6 us (0.07); the launches traced: 565 us -> 39.3 us
  matrix products: 207 us -> 0 us
  local copies, waits for them, and re-layouts: 196 us -> 3.71 us
  waiting for transfers between devices: 90.6 us -> 0 us
  other arithmetic: 35.3 us -> 0.08 us
  Pallas kernels: 0 us -> 34.8 us
  loops' own time: 19.4 us -> 0 us
  between operations: 16.3 us -> 0.71 us
    conv_general_dilated x24 -> x0, matrix products: 206 us -> none  [conv_volume(): lax.conv_general_dilated(padded[offset:offset + height], kernel[:, :, off...]
    psum x1 -> x0, waiting for transfers between devices: 90.6 us -> none  [spread(): return lax.psum(kept, axis)]
    conv_general_dilated x52 -> x0, local copies, waits for them, and re-layouts: 89.9 us -> none  [conv_volume(): lax.conv_general_dilated(padded[offset:offset + height], kernel[:, :, off...]
    convert_element_type x20 -> x0, local copies, waits for them, and re-layouts: 85.4 us -> none  [consensus_net(): hidden = jax.nn.relu(preact).astype(jnp.bfloat16)]
    pallas_call x0 -> x1, Pallas kernels: none -> 34.8 us  [per_device(): pl.pallas_call(functools.partial(kernel, n), out_shape=jax.ShapeDtypeStru...]
    conv_general_dilated x20 -> x0, other arithmetic: 19.8 us -> none  [conv_volume(): lax.conv_general_dilated(padded[offset:offset + height], kernel[:, :, off...]
    another operation x1 -> x0, loops' own time: 19.4 us -> none  [per_device(): filtered = lax.map(filter_one, volumes)]
    slice x25 -> x0, local copies, waits for them, and re-layouts: 15.2 us -> none  [the longest x24 13.8 us: conv_volume(): padded[offset:offset + height]]
  transfers between devices with their start and end apart: 1 -> 0, of which waited for: 1 -> 0; matrix products, arithmetic and copies ran while one was open for 0% -> 0% of each run, Pallas kernels for 0% -> 0%
where the time goes in v1:
time: 39.6 us; the launch traced here: 39.3 us
  Pallas kernels  34.8 us (88%)
  local copies, waits for them, and re-layouts  3.71 us (9%)
  between operations  0.71 us (2%)
    pallas_call x1, Pallas kernels, per_device(): pl.pallas_call(functools.partial(kernel, n), out_shape=jax.ShapeDtypeStru...  34.8 us
    unnamed x15, local copies, waits for them, and re-layouts  3.19 us

profile of v1, /device:TPU:31, one launch (start us, length us, event | category | flops | bytes accessed | tf_op | source)
XLA Modules:
  0.0 39.3 jit_solution(6708961753690733016)
XLA Ops:
  0.7 1.0 %copy.15 = bf16[16,1,3,3,3,3]{3,2,0,5,4,1:T(4,128)(2,1)S(1)} copy(bf16[16,1,3,3,3,3]{0,5,4,3,2,1:T(4,128)(2,1)} %param.12) | data formatting | bytes 5184 | tf_op args[4]
  1.7 0.0 copy-start.5
  1.7 0.2 reshape.6
  1.9 0.6 %copy-done.5 = bf16[1,16,3,3,3,3]{1,5,4,3,2,0:T(4,128)(2,1)S(1)} copy-done((bf16[1,16,3,3,3,3]{1,5,4,3,2,0:T(4,128)(2,1)S(1)}, bf16[1,16,3,3,3,3]{1,5,4,3,2,0:T(4,128)(2,1)}, u32[]{:S(2)}) %copy-start.5) | copy-done | bytes 2616
  2.4 0.0 copy-start
  2.4 0.0 copy-start.1
  2.4 0.3 copy.16
  2.7 0.2 reshape.7
  2.9 0.1 pad_maximum_fusion
  2.9 0.1 copy.17
  3.1 0.0 copy-start.2
  3.1 0.0 copy-start.3
  3.1 0.0 copy-start.4
  3.2 0.2 copy-done
  3.4 0.1 copy-done.1
  3.4 0.4 copy-done.2
  3.8 0.0 copy-done.3
  3.8 0.0 copy-done.4
  3.8 34.8 %consensus.1 = f32[1,2,128,128]{3,2,1,0:T(8,128)S(1)} custom-call(bf16[128,1024]{1,0:T(8,128)(2,1)S(1)} %copy-done, bf16[128,1024]{1,0:T(8,128)(2,1)S(1)} %copy-done.1, s32[4]{0:T(128)S(1)} %copy-done.2, s32[1,2]{1,0:T(1,128)S(1)} %copy-done.3, bf16[288,128]{1,0:T(8,128)(2,1)S(1)} %pad.4.taps_ref, f32[16]{0:T(128)S(1)} %copy-done.4, f32[1]{0:T(128)S(6)} %copy.19.b2_ref), custom_call_target="tpu_custom_call" | custom-call | tf_op jit(solution)/shard_map/consensus/pallas_call | solution.py:275
  38.6 0.7 %copy.20 = f32[1,2,128,128]{3,2,1,0:T(8,128)} copy(f32[1,2,128,128]{3,2,1,0:T(8,128)S(1)} %consensus.1) | data formatting | bytes 262144
  (1 shorter events, 0.0 us)
Async XLA Ops:
  1.7 0.7 %copy-start.5 = (bf16[1,16,3,3,3,3]{1,5,4,3,2,0:T(4,128)(2,1)S(1)}, bf16[1,16,3,3,3,3]{1,5,4,3,2,0:T(4,128)(2,1)}, u32[]{:S(2)}) copy-start(bf16[1,16,3,3,3,3]{1,5,4,3,2,0:T(4,128)(2,1)} %param.14) | copy-start | bytes 7780
  2.4 0.9 %copy-start = (bf16[128,1024]{1,0:T(8,128)(2,1)S(1)}, bf16[128,1024]{1,0:T(8,128)(2,1)}, u32[]{:S(2)}) copy-start(bf16[128,1024]{1,0:T(8,128)(2,1)} %q_ref.1) | copy-start | bytes 786436
  2.4 1.0 %copy-start.1 = (bf16[128,1024]{1,0:T(8,128)(2,1)S(1)}, bf16[128,1024]{1,0:T(8,128)(2,1)}, u32[]{:S(2)}) copy-start(bf16[128,1024]{1,0:T(8,128)(2,1)} %s_ref.1) | copy-start | bytes 786436
  3.1 0.7 %copy-start.2 = (s32[4]{0:T(128)S(1)}, s32[4]{0:T(128)}, u32[]{:S(2)}) copy-start(s32[4]{0:T(128)} %hubs_ref.1) | copy-start | bytes 52
  3.1 0.7 %copy-start.3 = (s32[1,2]{1,0:T(1,128)S(1)}, s32[1,2]{1,0:T(1,128)}, u32[]{:S(2)}) copy-start(s32[1,2]{1,0:T(1,128)} %pick_ref.1) | copy-start | bytes 28
  3.1 0.7 %copy-start.4 = (f32[16]{0:T(128)S(1)}, f32[16]{0:T(128)}, u32[]{:S(2)}) copy-start(f32[16]{0:T(128)} %b1_ref.1) | copy-start | bytes 196
